TPU v7x, 128 devices: a whole 4x4x4 slice. The times are simulated.
128 devices in a mesh: dp: 4 (over z), seq: 32 (over x, y, core).
Axes of the slice: x: 4, y: 4, z: 4, core: 2. Of those that a mesh axis runs over, the one named last changes fastest.
Arguments:
- image: bfloat16 [8, 192, 40, 256], P('dp', 'seq'), may hold values from -20 to 20
- embedding: bfloat16 [8, 512], P('dp'), may hold values from -6 to 6
- cotangent: bfloat16 [8, 192, 40, 256], P('dp', 'seq'), may hold values from -6 to 6
- valid_rows: int32 [8], P('dp'), may hold values from 48 to 192, as said below
- orientation: int32 [8], P('dp'), may hold values from 0 to 1
- gn1_gain: float32 [256], replicated, may hold values from 0.1 to 1.9
- gn1_bias: float32 [256], replicated, may hold values from -1.75 to 1.75
- conv1_weight: bfloat16 [3, 3, 256, 256], replicated, may hold values from -0.125 to 0.125
- conv1_bias: float32 [256], replicated, may hold values from -1.75 to 1.75
- time_weight: bfloat16 [512, 512], replicated, may hold values from -0.25 to 0.25
- time_bias: float32 [512], replicated, may hold values from -1.75 to 1.75
- gn2_gain: float32 [256], replicated, may hold values from 0.1 to 1.9
- gn2_bias: float32 [256], replicated, may hold values from -1.75 to 1.75
- conv2_weight: bfloat16 [3, 3, 256, 256], replicated, may hold values from -0.125 to 0.125
- conv2_bias: float32 [256], replicated, may hold values from -1.75 to 1.75
- gn3_gain: float32 [256], replicated, may hold values from 0.1 to 1.9
- gn3_bias: float32 [256], replicated, may hold values from -1.75 to 1.75
- qkv_weight: bfloat16 [256, 768], replicated, may hold values from -0.5 to 0.5
- qv_bias: float32 [512], replicated, may hold values from -1.75 to 1.75
- proj_weight: bfloat16 [256, 256], replicated, may hold values from -1.5 to 1.5
- proj_bias: float32 [256], replicated, may hold values from -1.75 to 1.75
Outputs:
- output: bfloat16 [8, 192, 40, 256], P('dp', 'seq')
- image_grad: bfloat16 [8, 192, 40, 256], P('dp', 'seq')
- embedding_grad: float32 [8, 512], P('dp')
- gn1_gain_grad: float32 [256], replicated
- gn1_bias_grad: float32 [256], replicated
- conv1_weight_grad: float32 [3, 3, 256, 256], replicated
- conv1_bias_grad: float32 [256], replicated
- time_weight_grad: float32 [512, 512], replicated
- time_bias_grad: float32 [512], replicated
- gn2_gain_grad: float32 [256], replicated
- gn2_bias_grad: float32 [256], replicated
- conv2_weight_grad: float32 [3, 3, 256, 256], replicated
- conv2_bias_grad: float32 [256], replicated
- gn3_gain_grad: float32 [256], replicated
- gn3_bias_grad: float32 [256], replicated
- qkv_weight_grad: float32 [256, 768], replicated
- qv_bias_grad: float32 [512], replicated
- proj_weight_grad: float32 [256, 256], replicated
- proj_bias_grad: float32 [256], replicated
Inputs may be any that keep to these rules, and one draw needn't show every extreme that they name: `valid_rows`: in every run of 2 consecutive images (one index of dp) one image has all 192 rows valid.
All inputs are finite; a program needn't handle non-finite values.
Results may differ from a plain program's by a relative error of at most 0.025.
The roundings to bfloat16 on the way count: a program that leaves them out, or rounds other values in their place, can miss the bound.
Values may be sent and summed in bfloat16 or wider, within the bound.
No kernel may reach another device: no remote copies, remote signals or barrier semaphores. Data moves between devices by JAX's collectives and lax.ppermute only.
A program may use at most 256 MiB of HBM per device.

v0:
```python
import jax
import jax.numpy as jnp
from jax import lax
from jax.sharding import PartitionSpec as P

GROUPS = 32
HEAD_COUNT = 4


EPS = 1e-05
LOWEST = -1e30


def padded_2(block, sides, width):
    for axis, dim in sides:
        count = lax.axis_size(axis)
        forward = [(i, i + 1) for i in range(count - 1)]
        backward = [(target, source) for source, target in forward]
        low = lax.ppermute(
            lax.slice_in_dim(block, block.shape[dim] - width, None, axis=dim), axis, forward
        )
        high = lax.ppermute(lax.slice_in_dim(block, 0, width, axis=dim), axis, backward)
        block = jnp.concatenate([low, block, high], axis=dim)
    return block


def silu_slope(values):
    sigmoid = jax.nn.sigmoid(values)
    return sigmoid * (1.0 + values * (1.0 - sigmoid))


def by_group(values):
    return values.reshape(values.shape[0], -1, GROUPS, values.shape[-1] // GROUPS)


def group_totals(first_part, second_part):
    return lax.psum((first_part, second_part), "seq")


def group_parts(values, normed):
    return (jnp.sum(by_group(values), axis=(1, 3)), jnp.sum(by_group(values * normed), axis=(1, 3)))


def norm_forward(values, valid_mask, counts):
    grouped = by_group(values)
    first_sum, second_sum = group_totals(
        jnp.sum(grouped, axis=(1, 3)), jnp.sum(grouped * grouped, axis=(1, 3))
    )
    average = first_sum / counts[:, None]
    spread = lax.rsqrt(second_sum / counts[:, None] - average * average + EPS)
    normed = (grouped - average[:, None, :, None]) * spread[:, None, :, None]
    return (valid_mask * normed.reshape(values.shape), spread)


def norm_input_grad(grad_hat, normed, spread, valid_mask, counts, first_sum, second_sum):
    first_mean = (first_sum / counts[:, None])[:, None, :, None]
    second_mean = (second_sum / counts[:, None])[:, None, :, None]
    result = spread[:, None, :, None] * (
        by_group(grad_hat) - first_mean - by_group(normed) * second_mean
    )
    return valid_mask * result.reshape(grad_hat.shape)


def patches(padded, shard_rows, columns):
    widened = jnp.pad(padded, ((0, 0), (0, 0), (1, 1), (0, 0)))
    return jnp.concatenate(
        [
            widened[:, row_off : row_off + shard_rows, col_off : col_off + columns, :]
            for row_off in range(3)
            for col_off in range(3)
        ],
        axis=-1,
    )


def conv_forward(active, weight):
    padded = padded_2(active, (("seq", 1),), 1)
    gathered = patches(padded, active.shape[1], active.shape[2])
    flat_weight = weight.reshape(-1, weight.shape[-1])
    return (jnp.dot(gathered, flat_weight, preferred_element_type=jnp.float32), gathered)


def conv_backward(grad_low, gathered, weight):
    weight_grad = jnp.einsum(
        "nrwk,nrwo->ko", gathered, grad_low, preferred_element_type=jnp.float32
    ).reshape(weight.shape)
    bias_grad = jnp.sum(grad_low, axis=(0, 1, 2), dtype=jnp.float32)
    padded = padded_2(grad_low, (("seq", 1),), 1)
    flipped = jnp.transpose(weight[::-1, ::-1], (0, 1, 3, 2)).reshape(-1, weight.shape[-1])
    input_grad = jnp.dot(
        patches(padded, grad_low.shape[1], grad_low.shape[2]),
        flipped,
        preferred_element_type=jnp.float32,
    )
    return (input_grad, weight_grad, bias_grad)


def key_valid(first_row, length, valid_rows, col_valid, columns):
    positions = first_row + jnp.arange(length, dtype=jnp.int32)
    row_ok = (positions // columns)[None, :] < valid_rows[:, None]
    col_ok = (positions % columns)[None, :] < col_valid[:, None]
    return row_ok & col_ok


def split_heads(values):
    return values.reshape(values.shape[0], values.shape[1], HEAD_COUNT, -1)


def attend_piece(carried, pieces, first_row, query_heads, valid_rows, col_valid, columns):
    maxima, totals, accumulated = carried
    key_heads = split_heads(pieces[0])
    value_heads = split_heads(pieces[1])
    keymask = key_valid(first_row, key_heads.shape[1], valid_rows, col_valid, columns)[
        :, None, None, :
    ]
    factor = query_heads.shape[-1] ** (-0.5)
    scores = (
        jnp.einsum("iqhd,ikhd->ihqk", query_heads, key_heads, preferred_element_type=jnp.float32)
        * factor
    )
    scores = jnp.where(keymask, scores, LOWEST)
    new_max = jnp.maximum(maxima, jnp.max(scores, axis=-1))
    weights = jnp.where(keymask, jnp.exp(scores - new_max[..., None]), 0.0)
    totals = jnp.sum(weights, axis=-1)
    accumulated = jnp.einsum(
        "ihqk,ikhd->ihqd",
        weights.astype(jnp.bfloat16),
        value_heads,
        preferred_element_type=jnp.float32,
    )
    return (new_max, totals, accumulated)


def full_grads(query_heads, grad_heads, key_heads, value_heads, keymask, logsum, delta_rows):
    factor = query_heads.shape[-1] ** (-0.5)
    scores = (
        jnp.einsum("iqhd,ikhd->ihqk", query_heads, key_heads, preferred_element_type=jnp.float32)
        * factor
    )
    scores = jnp.where(keymask, scores, LOWEST)
    weights = jnp.where(keymask, jnp.exp(scores - logsum[..., None]), 0.0)
    weight_grad = jnp.einsum(
        "iqhd,ikhd->ihqk", grad_heads, value_heads, preferred_element_type=jnp.float32
    )
    score_grad = (weights * (weight_grad - delta_rows[..., None]) * factor).astype(jnp.bfloat16)
    return (weights.astype(jnp.bfloat16), score_grad)


def per_device(
    image,
    embedding,
    cotangent,
    valid_rows,
    orientation,
    gn1_gain,
    gn1_bias,
    conv1_weight,
    conv1_bias,
    time_weight,
    time_bias,
    gn2_gain,
    gn2_bias,
    conv2_weight,
    conv2_bias,
    gn3_gain,
    gn3_bias,
    qkv_weight,
    qv_bias,
    proj_weight,
    proj_bias,
):
    images, shard_rows, columns, channels = image.shape
    tokens = shard_rows * columns
    head_width = channels // HEAD_COUNT
    seq_index = lax.axis_index("seq")
    row_ids = seq_index * shard_rows + jnp.arange(shard_rows, dtype=jnp.int32)
    col_valid = columns - 2 * columns // 5 * orientation
    pixel_ok = (row_ids[None, :, None] < valid_rows[:, None, None]) & (
        jnp.arange(columns, dtype=jnp.int32)[None, None, :] < col_valid[:, None, None]
    )
    valid_mask = pixel_ok.astype(jnp.float32)[..., None]
    counts = (valid_rows * col_valid).astype(jnp.float32) * (channels // GROUPS)
    masked_input = valid_mask * image.astype(jnp.float32)
    first_hat, first_spread = norm_forward(masked_input, valid_mask, counts)
    first_norm = valid_mask * (first_hat * gn1_gain + gn1_bias)
    first_active = jax.nn.silu(first_norm).astype(jnp.bfloat16)
    first_conv, first_patch = conv_forward(first_active, conv1_weight)
    hidden = valid_mask * (first_conv + conv1_bias)
    time_input = jax.nn.silu(embedding.astype(jnp.float32)).astype(jnp.bfloat16)
    shifts = jnp.dot(time_input, time_weight, preferred_element_type=jnp.float32) + time_bias
    scaling = shifts[:, None, None, :channels]
    offset = shifts[:, None, None, channels:]
    second_hat, second_spread = norm_forward(hidden, valid_mask, counts)
    second_base = valid_mask * (second_hat * gn2_gain + gn2_bias)
    second_norm = valid_mask * (second_base * (1.0 + scaling) + offset)
    second_active = jax.nn.silu(second_norm).astype(jnp.bfloat16)
    second_conv, second_patch = conv_forward(second_active, conv2_weight)
    residual = masked_input + valid_mask * (second_conv + conv2_bias)
    third_hat, third_spread = norm_forward(residual, valid_mask, counts)
    third_low = (
        (valid_mask * (third_hat * gn3_gain + gn3_bias))
        .astype(jnp.bfloat16)
        .reshape(images, tokens, channels)
    )
    mixture = jnp.dot(third_low, qkv_weight, preferred_element_type=jnp.float32)
    queries = (mixture[..., :channels] + qv_bias[:channels]).astype(jnp.bfloat16)
    keys_low = mixture[..., channels : 2 * channels].astype(jnp.bfloat16)
    values_low = (mixture[..., 2 * channels :] + qv_bias[channels:]).astype(jnp.bfloat16)
    query_heads = split_heads(queries)
    initial = (
        jnp.full((images, HEAD_COUNT, tokens), LOWEST, jnp.float32),
        jnp.zeros((images, HEAD_COUNT, tokens), jnp.float32),
        jnp.zeros((images, HEAD_COUNT, tokens, head_width), jnp.float32),
    )
    maxima, totals, accumulated = attend_piece(
        initial,
        (
            lax.all_gather(keys_low, "seq", axis=1, tiled=True),
            lax.all_gather(values_low, "seq", axis=1, tiled=True),
        ),
        jnp.int32(0),
        query_heads,
        valid_rows,
        col_valid,
        columns,
    )
    attended = jnp.transpose(accumulated / totals[..., None], (0, 2, 1, 3))
    logsum = maxima + jnp.log(totals)
    attended_low = attended.reshape(images, tokens, channels).astype(jnp.bfloat16)
    projected = jnp.dot(attended_low, proj_weight, preferred_element_type=jnp.float32) + proj_bias
    output = (residual + valid_mask * projected.reshape(residual.shape)).astype(jnp.bfloat16)
    cotan_full = cotangent.astype(jnp.float32)
    proj_grad = (valid_mask * cotan_full).astype(jnp.bfloat16).reshape(images, tokens, channels)
    proj_weight_grad = jnp.einsum(
        "itc,itd->cd", attended_low, proj_grad, preferred_element_type=jnp.float32
    )
    proj_bias_grad = jnp.sum(proj_grad, axis=(0, 1), dtype=jnp.float32)
    attended_grad = jnp.einsum(
        "itd,cd->itc", proj_grad, proj_weight, preferred_element_type=jnp.float32
    ).astype(jnp.bfloat16)
    grad_heads = split_heads(attended_grad)
    delta_rows = jnp.transpose(
        jnp.sum(grad_heads.astype(jnp.float32) * attended, axis=-1), (0, 2, 1)
    )
    every_key, every_value = (
        lax.all_gather(keys_low, "seq", axis=1, tiled=True),
        lax.all_gather(values_low, "seq", axis=1, tiled=True),
    )
    every_key_heads = split_heads(every_key)
    every_value_heads = split_heads(every_value)
    all_mask = key_valid(0, every_key.shape[1], valid_rows, col_valid, columns)[:, None, None, :]
    weights_low, score_grad = full_grads(
        query_heads, grad_heads, every_key_heads, every_value_heads, all_mask, logsum, delta_rows
    )
    query_grad = (
        jnp.einsum(
            "ihqk,ikhd->iqhd", score_grad, every_key_heads, preferred_element_type=jnp.float32
        )
        .astype(jnp.bfloat16)
        .reshape(images, tokens, channels)
    )
    key_term = jnp.einsum(
        "ihqk,iqhd->kihd", score_grad, query_heads, preferred_element_type=jnp.float32
    )
    value_term = jnp.einsum(
        "ihqk,iqhd->kihd", weights_low, grad_heads, preferred_element_type=jnp.float32
    )
    term_rows = jnp.transpose(
        lax.psum_scatter(
            jnp.concatenate([key_term, value_term], axis=2)
            .reshape(tokens * lax.axis_size("seq"), images, 2 * channels)
            .astype(jnp.bfloat16),
            "seq",
            scatter_dimension=0,
            tiled=True,
        ).astype(jnp.float32),
        (1, 0, 2),
    )
    key_grad = term_rows[..., :channels].astype(jnp.bfloat16)
    value_grad = term_rows[..., channels:].astype(jnp.bfloat16)
    mixture_grad = jnp.concatenate([query_grad, key_grad, value_grad], axis=-1)
    third_grad = jnp.einsum(
        "itk,ck->itc", mixture_grad, qkv_weight, preferred_element_type=jnp.float32
    ).reshape(residual.shape)
    qkv_weight_grad = jnp.einsum(
        "itc,itk->ck", third_low, mixture_grad, preferred_element_type=jnp.float32
    )
    qv_bias_grad = jnp.concatenate(
        [
            jnp.sum(query_grad, axis=(0, 1), dtype=jnp.float32),
            jnp.sum(value_grad, axis=(0, 1), dtype=jnp.float32),
        ]
    )
    third_up = valid_mask * third_grad
    gn3_gain_grad = jnp.sum(third_up * third_hat, axis=(0, 1, 2))
    gn3_bias_grad = jnp.sum(third_up, axis=(0, 1, 2))
    third_dhat = third_up * gn3_gain
    first_part, second_part = group_parts(third_dhat, third_hat)
    first_sum, second_sum = group_totals(first_part, second_part)
    residual_grad = cotan_full + norm_input_grad(
        third_dhat, third_hat, third_spread, valid_mask, counts, first_sum, second_sum
    )
    branch_low = (valid_mask * residual_grad).astype(jnp.bfloat16)
    active2_grad, conv2_weight_grad, conv2_bias_grad = conv_backward(
        branch_low, second_patch, conv2_weight
    )
    norm2_grad = valid_mask * active2_grad * silu_slope(second_norm)
    scale_part = jnp.sum(norm2_grad * second_base, axis=(1, 2))
    offset_part = jnp.sum(norm2_grad, axis=(1, 2))
    base_grad = norm2_grad * (1.0 + scaling)
    gn2_gain_grad = jnp.sum(base_grad * second_hat, axis=(0, 1, 2))
    gn2_bias_grad = jnp.sum(base_grad, axis=(0, 1, 2))
    second_dhat = base_grad * gn2_gain
    first_part, second_part = group_parts(second_dhat, second_hat)
    first_sum, second_sum, scale_total, offset_total = lax.psum(
        (first_part, second_part, scale_part, offset_part), "seq"
    )
    hidden_grad = norm_input_grad(
        second_dhat, second_hat, second_spread, valid_mask, counts, first_sum, second_sum
    )
    shift_low = jnp.concatenate([scale_total, offset_total], axis=-1).astype(jnp.bfloat16)
    first_seq = seq_index == 0
    time_weight_grad = jnp.where(
        first_seq,
        jnp.einsum("ie,ik->ek", time_input, shift_low, preferred_element_type=jnp.float32),
        0.0,
    )
    time_bias_grad = jnp.where(first_seq, jnp.sum(shift_low, axis=0, dtype=jnp.float32), 0.0)
    embedding_grad = jnp.einsum(
        "ik,ek->ie", shift_low, time_weight, preferred_element_type=jnp.float32
    ) * silu_slope(embedding.astype(jnp.float32))
    hidden_low = (valid_mask * hidden_grad).astype(jnp.bfloat16)
    active1_grad, conv1_weight_grad, conv1_bias_grad = conv_backward(
        hidden_low, first_patch, conv1_weight
    )
    norm1_grad = valid_mask * active1_grad * silu_slope(first_norm)
    gn1_gain_grad = jnp.sum(norm1_grad * first_hat, axis=(0, 1, 2))
    gn1_bias_grad = jnp.sum(norm1_grad, axis=(0, 1, 2))
    first_dhat = norm1_grad * gn1_gain
    first_part, second_part = group_parts(first_dhat, first_hat)
    first_sum, second_sum = group_totals(first_part, second_part)
    input_grad = residual_grad + norm_input_grad(
        first_dhat, first_hat, first_spread, valid_mask, counts, first_sum, second_sum
    )
    image_grad = (valid_mask * input_grad).astype(jnp.bfloat16)
    summed = lax.psum(
        (
            gn1_gain_grad,
            gn1_bias_grad,
            conv1_weight_grad,
            conv1_bias_grad,
            time_weight_grad,
            time_bias_grad,
            gn2_gain_grad,
            gn2_bias_grad,
            conv2_weight_grad,
            conv2_bias_grad,
            gn3_gain_grad,
            gn3_bias_grad,
            qkv_weight_grad,
            qv_bias_grad,
            proj_weight_grad,
            proj_bias_grad,
        ),
        ("dp", "seq"),
    )
    return (output, image_grad, embedding_grad) + tuple(summed)


def solution(mesh):
    return jax.shard_map(
        per_device,
        mesh=mesh,
        in_specs=(
            P("dp", "seq", None, None),
            P("dp", None),
            P("dp", "seq", None, None),
            P("dp"),
            P("dp"),
            P(),
            P(),
            P(),
            P(),
            P(),
            P(),
            P(),
            P(),
            P(),
            P(),
            P(),
            P(),
            P(),
            P(),
            P(),
            P(),
        ),
        out_specs=(
            P("dp", "seq", None, None),
            P("dp", "seq", None, None),
            P("dp", None),
            P(),
            P(),
            P(),
            P(),
            P(),
            P(),
            P(),
            P(),
            P(),
            P(),
            P(),
            P(),
            P(),
            P(),
            P(),
            P(),
        ),
        check_vma=False,
    )
```

profile of v0, /device:TPU:1, one launch (start us, length us, event | category | flops | bytes accessed | tf_op | source)
XLA Modules:
  0.0 987.8 jit_solution(7909394192991495609)
XLA Ops:
  7.3 0.7 multiply_subtract_fusion
  8.7 0.7 broadcast_compare_fusion
  9.6 1.2 multiply_reduce_fusion.11
  11.1 63.8 %all-reduce.11 = (f32[2,32]{1,0:T(2,128)S(1)}, f32[2,32]{1,0:T(2,128)S(1)}) all-reduce(f32[2,32]{1,0:T(2,128)S(1)} %reduce_sum.281, f32[2,32]{1,0:T(2,128)S(1)} %reduce_sum.287), channel_id=1, replica_groups=mesh['dp'=4,'seq'=32] {'seq'}, use_global_device_ids=true, to_apply=%region_2.0 | all-reduce | flops 128 | bytes 1024 | tf_op jit(solution)/shard_map/psum | solution.py:37
  75.3 1.3 multiply_convert_fusion.6
  76.6 3.0 collective-permute-start
  79.6 5.2 collective-permute-start.1
  84.8 0.9 convolution_add_fusion.3
  87.2 0.8 multiply_reduce_fusion.10
  88.4 62.3 %all-reduce.10 = (f32[2,32]{1,0:T(2,128)S(1)}, f32[2,32]{1,0:T(2,128)S(1)}) all-reduce(f32[2,32]{1,0:T(2,128)S(1)} %reduce_sum.346, f32[2,32]{1,0:T(2,128)S(1)} %reduce_sum.349), channel_id=1, replica_groups=mesh['dp'=4,'seq'=32] {'seq'}, use_global_device_ids=true, to_apply=%region_8.9 | all-reduce | flops 128 | bytes 1024 | tf_op jit(solution)/shard_map/psum | solution.py:37
  151.4 1.9 collective-permute-start.2
  153.4 2.4 collective-permute-start.3
  155.8 2.9 collective-permute-done.3
  160.1 0.8 multiply_reduce_fusion.9
  161.3 60.3 %all-reduce.9 = (f32[2,32]{1,0:T(2,128)S(1)}, f32[2,32]{1,0:T(2,128)S(1)}) all-reduce(f32[2,32]{1,0:T(2,128)S(1)} %reduce_sum.352, f32[2,32]{1,0:T(2,128)S(1)} %reduce_sum.355), channel_id=1, replica_groups=mesh['dp'=4,'seq'=32] {'seq'}, use_global_device_ids=true, to_apply=%region_14.15 | all-reduce | flops 128 | bytes 1024 | tf_op jit(solution)/shard_map/psum | solution.py:37
  222.1 0.8 convert_reduce_fusion.1
  222.9 0.7 copy-done.21
  224.0 0.7 slice.292
  224.8 0.8 fusion.36
  226.4 50.1 %all-gather.3.cloned.1.call-done = bf16[2,7680,256]{2,1,0:T(8,128)(2,1)} async-done(((bf16[2,240,256]{2,1,0:T(8,128)(2,1)}), bf16[2,7680,256]{2,1,0:T(8,128)(2,1)}) %all-gather.3.cloned.1.call-update) | async-done | bytes 7864336 | tf_op jit(solution)/shard_map/all_gather | solution.py:218
  276.4 10.9 %copy.64 = bf16[2,7680,256]{1,2,0:T(8,128)(2,1)} copy(bf16[2,7680,256]{2,1,0:T(8,128)(2,1)} %all-gather.3.cloned.1.call-done) | data formatting | bytes 15728640 | tf_op jit(solution)/shard_map/all_gather | solution.py:218
  287.3 24.7 %fusion.3 = (f32[2,4,240]{2,1,0:T(4,128)S(1)}, f32[2,4,240,7680]{3,2,1,0:T(8,128)}) fusion(pred[2,7680]{1,0:T(4,128)(4,1)S(1)} %compare_and_fusion, bf16[2,240,4,64]{1,3,2,0:T(8,128)(2,1)S(1)} %bitcast.122, bf16[2,7680,4,64]{1,3,2,0:T(8,128)(2,1)} %bitcast.113), kind=kOutput, calls=%fused_computation.7 | convolution fusion | flops 1931671680 | bytes 67115520 | tf_op jit(solution)/shard_map/iqhd,ikhd->ihqk/dot_general | solution.py:118
  312.0 21.0 %fusion = f32[2,4,240]{2,1,0:T(4,128)S(1)} fusion(f32[2,4,240,7680]{3,2,1,0:T(8,128)} %get-tuple-element.109, f32[2,4,240]{2,1,0:T(4,128)S(1)} %broadcast_maximum_fusion, pred[2,7680]{1,0:T(4,128)(4,1)S(1)} %compare_and_fusion), kind=kLoop, calls=%fused_computation.4 | loop fusion | flops 73726080 | bytes 59013120 | tf_op jit(solution)/shard_map/reduce_sum | solution.py:124
  333.1 10.4 %copy.65 = bf16[2,7680,256]{1,2,0:T(8,128)(2,1)} copy(bf16[2,7680,256]{2,1,0:T(8,128)(2,1)} %all-gather.5.cloned.1.call-done) | data formatting | bytes 15728640 | tf_op jit(solution)/shard_map/all_gather | solution.py:219
  343.5 23.6 %multiply_reduce_fusion = (f32[2,240,4]{1,2,0:T(4,128)S(1)}, bf16[2,240,4,64]{1,3,2,0:T(8,128)(2,1)S(1)}) fusion(bf16[2,240,256]{1,2,0:T(8,128)(2,1)S(1)} %copy.67, f32[2,240,4]{1,2,0:T(4,128)S(1)} %bitcast.142, bf16[2,7680,4,64]{1,3,2,0:T(8,128)(2,1)} %bitcast.116, f32[2,4,240,7680]{3,2,1,0:T(8,128)} %get-tuple-element.109, ...), kind=kOutput, calls=%fused_computation.46 | convolution fusion | flops 1961777280 | bytes 67376640 | tf_op jit(solution)/shard_map/ihqk,ikhd->ihqd/dot_general | solution.py:125
  367.1 25.9 %fusion.14 = bf16[7680,2,4,64]{0,3,2,1:T(8,128)(2,1)} fusion(bf16[2,240,4,64]{1,3,2,0:T(8,128)(2,1)S(1)} %bitcast.137, f32[2,4,240,7680]{3,2,1,0:T(8,128)} %get-tuple-element.109, f32[2,4,240]{2,1,0:T(4,128)S(1)} %log_add_fusion, pred[2,7680]{1,0:T(4,128)(4,1)S(1)} %compare_and_fusion), kind=kOutput, calls=%fused_computation.16 | convolution fusion | flops 1965096960 | bytes 67115520 | tf_op jit(solution)/shard_map/ihqk,iqhd->kihd/dot_general | solution.py:265
  393.0 39.7 %multiply_convert_fusion = bf16[2,4,240,7680]{3,2,1,0:T(8,128)(2,1)} fusion(f32[2,4,240,7680]{3,2,1,0:T(8,128)} %get-tuple-element.109, f32[2,4,240]{2,1,0:T(4,128)S(1)} %bitcast.143, f32[2,4,240]{2,1,0:T(4,128)S(1)} %log_add_fusion, pred[2,7680]{1,0:T(4,128)(4,1)S(1)} %compare_and_fusion, bf16[2,240,4,64]{1,3,2,0:T(8,128)(2,1)S(1)} %bitcast.138, ...), kind=kOutput, calls=%fused_computation | convolution fusion | flops 2005401600 | bytes 96614400 | tf_op jit(solution)/shard_map/iqhd,ikhd->ihqk/dot_general | solution.py:142
  432.7 17.8 %fusion.13 = bf16[7680,2,4,64]{0,3,2,1:T(8,128)(2,1)} fusion(bf16[2,240,4,64]{1,3,2,0:T(8,128)(2,1)S(1)} %bitcast.123, bf16[2,4,240,7680]{3,2,1,0:T(8,128)(2,1)} %multiply_convert_fusion), kind=kOutput, calls=%fused_computation.15 | convolution fusion | flops 1891368960 | bytes 37601280 | tf_op jit(solution)/shard_map/ihqk,iqhd->kihd/dot_general | solution.py:262
  450.5 13.2 %pad_maximum_fusion = bf16[7680,2,8,64]{0,3,2,1:T(8,128)(2,1)} fusion(bf16[7680,2,4,64]{0,3,2,1:T(8,128)(2,1)} %fusion.14, bf16[7680,2,4,64]{0,3,2,1:T(8,128)(2,1)} %fusion.13), kind=kLoop, calls=%fused_computation.12 | loop fusion | flops 7864320 | bytes 31457280 | tf_op jit(solution)/shard_map/concatenate | solution.py:270
  463.7 20.7 %copy.68 = bf16[7680,2,512]{2,0,1:T(8,128)(2,1)} copy(bf16[7680,2,512]{0,2,1:T(8,128)(2,1)} %bitcast.115) | data formatting | bytes 31457280 | tf_op jit(solution)/shard_map/convert_element_type | solution.py:272
  485.7 1.0 copy.70
  486.6 1.6 copy.71
  488.2 1.1 rev.6
  489.3 1.2 rev.7
  490.5 6.9 dot_general.88
  497.4 18.8 %convert_reduce_fusion = (f32[4,64]{1,0:T(4,128)S(1)}, bf16[2,4,64,240]{3,2,1,0:T(8,128)(2,1)S(1)}) fusion(bf16[2,7680,4,64]{1,3,2,0:T(8,128)(2,1)} %bitcast.114, bf16[2,4,240,7680]{3,2,1,0:T(8,128)(2,1)} %multiply_convert_fusion), kind=kOutput, calls=%fused_computation.45 | convolution fusion | flops 1887805184 | bytes 37602304 | tf_op jit(solution)/shard_map/ihqk,ikhd->iqhd/dot_general | solution.py:256
  516.5 1.0 convolution_bitcast_fusion.1
  517.4 77.3 %reduce-scatter.2.cloned.1.call-done = bf16[240,2,512]{2,0,1:T(8,128)(2,1)} async-done(((bf16[7680,2,512]{2,0,1:T(8,128)(2,1)}), bf16[240,2,512]{2,0,1:T(8,128)(2,1)}) %reduce-scatter.2.cloned.1.call-update) | async-done | bytes 491536 | tf_op jit(solution)/shard_map/reduce_scatter | solution.py:269
  594.7 1.5 multiply_reduce_fusion.12
  596.8 64.2 %all-reduce.8 = (f32[2,32]{1,0:T(2,128)S(1)}, f32[2,32]{1,0:T(2,128)S(1)}) all-reduce(f32[2,32]{1,0:T(2,128)S(1)} %reduce_sum.363, f32[2,32]{1,0:T(2,128)S(1)} %reduce_sum.360), channel_id=1, replica_groups=mesh['dp'=4,'seq'=32] {'seq'}, use_global_device_ids=true, to_apply=%region_27.28 | all-reduce | flops 128 | bytes 1024 | tf_op jit(solution)/shard_map/psum | solution.py:37
  661.8 4.0 fusion.89
  665.8 1.9 collective-permute-start.4
  667.7 2.7 collective-permute-start.5
  670.4 1.3 convolution_bitcast_fusion
  671.7 1.3 collective-permute-done.5
  674.6 1.1 multiply_reduce_fusion.2
  676.1 60.6 %all-reduce.7 = (f32[2,32]{1,0:T(2,128)S(1)}, f32[2,32]{1,0:T(2,128)S(1)}) all-reduce(f32[2,32]{1,0:T(2,128)S(1)} %reduce_sum.369, f32[2,32]{1,0:T(2,128)S(1)} %reduce_sum.366), channel_id=1, replica_groups=mesh['dp'=4,'seq'=32] {'seq'}, use_global_device_ids=true, to_apply=%region_33.34 | all-reduce | flops 128 | bytes 1024 | tf_op jit(solution)/shard_map/psum | solution.py:315
  737.4 1.9 collective-permute-start.6
  739.3 3.8 collective-permute-start.7
  743.2 4.1 fusion.19
  748.9 1.8 multiply_reduce_fusion.3
  751.1 62.4 %all-reduce.6 = (f32[2,32]{1,0:T(2,128)S(1)}, f32[2,32]{1,0:T(2,128)S(1)}, bf16[2,256]{1,0:T(2,128)(2,1)S(1)}, bf16[2,256]{1,0:T(2,128)(2,1)S(1)}) all-reduce(f32[2,32]{1,0:T(2,128)S(1)} %reduce_sum.375, f32[2,32]{1,0:T(2,128)S(1)} %reduce_sum.372, f32[2,256]{1,0:T(2,128)S(1)} %get-tuple-element.31, ...), channel_id=1, replica_groups=mesh['dp'=4,'seq'=32] {'seq'}, use_global_device_ids=true, to_apply=%region_39.40 | all-reduce | flops 1152 | bytes 7168 | tf_op jit(solution)/shard_map/psum | solution.py:37
  813.4 1.3 convolution_select_fusion
  814.9 0.8 copy-done.25
  815.9 1.0 convert_reduce_fusion.2
  817.4 65.2 %all-reduce.4 = (f32[256]{0:T(256)}, f32[256]{0:T(256)}, f32[256]{0:T(256)}, f32[512]{0:T(512)}, f32[256]{0:T(256)}, /*index=5*/f32[256]{0:T(256)}, f32[256]{0:T...) all-reduce(f32[256]{0:T(256)S(1)} %get-tuple-element.24, ...), channel_id=1, replica_groups=mesh['dp'=4,'seq'=32] {'dp','seq'}, use_global_device_ids=true, to_apply=%region_45.46 | all-reduce | flops 3328 | bytes 26624 | tf_op jit(solution)/shard_map/psum | solution.py:346
  882.6 0.8 convolution_multiply_fusion.2
  883.5 2.3 multiply_convert_fusion.1
  885.8 87.4 %all-reduce.14.cloned.1.call-done = (f32[3,3,256,256]{3,2,1,0:T(8,128)}, f32[512,512]{1,0:T(8,128)}, f32[3,3,256,256]{3,2,1,0:T(8,128)}, f32[256,768]{1,0:T(8,128)}, f32[256,256]{1,0:T(8,128)}) async-done(((f32[3,3,256,256]{3,2,1,0:T(8,128)}, f32[512,512]{1,0:T(8,128)}, f32[3,3,256,256]{3,2,1,0:T(8,128)}, f32[256,768]{1,0:T(8,128)}, f32[256,256]{1,0:T(8,128)}), (f32[3,3,256,256]{3,2,1,0:T(8,128)}, ...) | async-done | bytes 6815760 | tf_op jit(solution)/shard_map/psum | solution.py:346
  973.2 3.4 copy.124
  976.6 1.0 copy.125
  977.6 1.4 copy.126
  979.3 0.9 copy.127
  980.1 0.7 copy.128
  (270 shorter events, 15.5 us)
Async XLA Ops:
  7.2 77.6 %copy-start = (bf16[512,512]{1,0:T(8,128)(2,1)S(1)}, bf16[512,512]{1,0:T(8,128)(2,1)}, u32[]{:S(2)}) copy-start(bf16[512,512]{1,0:T(8,128)(2,1)} %param.30) | copy-start | bytes 1572868
  7.2 269.2 %all-gather.3.cloned.1.call-start = ((), (), s32[]{:S(2)}) async-start(), calls=%async_computation.1 | async-start | bytes 8110080 | tf_op jit(solution)/shard_map/all_gather | solution.py:218
  8.7 213.0 %copy-start.48 = (f32[2]{0:T(128)}, f32[2]{0:T(128)S(1)}, u32[]{:S(2)}) copy-start(f32[2]{0:T(128)S(1)} %convert_multiply_fusion.4) | copy-start | bytes 28
  9.5 212.6 %copy-start.13 = (f32[2,6,40]{2,1,0:T(8,128)}, f32[2,6,40]{2,1,0:T(8,128)S(1)}, u32[]{:S(2)}) copy-start(f32[2,6,40]{2,1,0:T(8,128)S(1)} %and_convert_fusion) | copy-start | bytes 5764
  9.5 76.5 %copy-start.5 = (bf16[2,6,40,256]{3,2,1,0:T(8,128)(2,1)S(1)}, bf16[2,6,40,256]{3,2,1,0:T(8,128)(2,1)}, u32[]{:S(2)}) copy-start(bf16[2,6,40,256]{3,2,1,0:T(8,128)(2,1)} %param.21) | copy-start | bytes 737284
  9.5 76.5 %copy-start.52 = (f32[256]{0:T(256)S(1)}, f32[256]{0:T(256)}, u32[]{:S(2)}) copy-start(f32[256]{0:T(256)} %param.26) | copy-start | bytes 3076
  9.5 76.6 %copy-start.58 = (f32[256]{0:T(256)S(1)}, f32[256]{0:T(256)}, u32[]{:S(2)}) copy-start(f32[256]{0:T(256)} %param.27) | copy-start | bytes 3076
  75.1 11.3 %copy-start.34 = (f32[2,256]{1,0:T(2,128)}, f32[2,256]{1,0:T(2,128)S(1)}, u32[]{:S(2)}) copy-start(f32[2,256]{1,0:T(2,128)S(1)} %mul.412) | copy-start | bytes 6148
  75.3 11.1 %copy-start.36 = (f32[2,256]{1,0:T(2,128)}, f32[2,256]{1,0:T(2,128)S(1)}, u32[]{:S(2)}) copy-start(f32[2,256]{1,0:T(2,128)S(1)} %sub.145) | copy-start | bytes 6148
  76.6 9.1 collective-permute-start
  79.6 6.2 collective-permute-start.1
  85.7 73.3 %copy-start.42 = (f32[2,256]{1,0:T(2,128)}, f32[2,256]{1,0:T(2,128)S(1)}, u32[]{:S(2)}) copy-start(f32[2,256]{1,0:T(2,128)S(1)} %get-tuple-element.96) | copy-start | bytes 6148
  85.7 73.3 %copy-start.46 = (f32[2,256]{1,0:T(2,128)}, f32[2,256]{1,0:T(2,128)S(1)}, u32[]{:S(2)}) copy-start(f32[2,256]{1,0:T(2,128)S(1)} %get-tuple-element.97) | copy-start | bytes 6148
  87.2 63.9 %copy-start.54 = (f32[256]{0:T(256)S(1)}, f32[256]{0:T(256)}, u32[]{:S(2)}) copy-start(f32[256]{0:T(256)} %param.32) | copy-start | bytes 3076
  87.2 63.9 %copy-start.56 = (f32[256]{0:T(256)S(1)}, f32[256]{0:T(256)}, u32[]{:S(2)}) copy-start(f32[256]{0:T(256)} %param.33) | copy-start | bytes 3076
  88.0 71.3 %copy-start.3 = (f32[2,6,40,256]{3,2,1,0:T(8,128)}, f32[2,6,40,256]{3,2,1,0:T(8,128)S(1)}, u32[]{:S(2)}) copy-start(f32[2,6,40,256]{3,2,1,0:T(8,128)S(1)} %get-tuple-element.106) | copy-start | bytes 1474564
  150.9 8.4 copy-start.38
  151.1 8.3 copy-start.40
  151.4 4.3 collective-permute-start.2
  153.4 5.3 collective-permute-start.3
  159.6 1.4 copy-start.44
  160.1 62.0 %copy-start.9 = (bf16[2,6,40,256]{3,2,1,0:T(8,128)(2,1)S(1)}, bf16[2,6,40,256]{3,2,1,0:T(8,128)(2,1)}, u32[]{:S(2)}) copy-start(bf16[2,6,40,256]{3,2,1,0:T(8,128)(2,1)} %param.23) | copy-start | bytes 737284
  160.1 62.0 %copy-start.50 = (f32[256]{0:T(256)S(1)}, f32[256]{0:T(256)}, u32[]{:S(2)}) copy-start(f32[256]{0:T(256)} %param.36) | copy-start | bytes 3076
  160.1 62.0 %copy-start.62 = (f32[256]{0:T(256)S(1)}, f32[256]{0:T(256)}, u32[]{:S(2)}) copy-start(f32[256]{0:T(256)} %param.37) | copy-start | bytes 3076
  160.1 63.5 %copy-start.26 = (bf16[256,768]{1,0:T(8,128)(2,1)S(1)}, bf16[256,768]{1,0:T(8,128)(2,1)}, u32[]{:S(2)}) copy-start(bf16[256,768]{1,0:T(8,128)(2,1)} %param.38) | copy-start | bytes 1179652
  160.9 64.6 %copy-start.1 = (f32[2,6,40,256]{3,2,1,0:T(8,128)}, f32[2,6,40,256]{3,2,1,0:T(8,128)S(1)}, u32[]{:S(2)}) copy-start(f32[2,6,40,256]{3,2,1,0:T(8,128)S(1)} %get-tuple-element.107) | copy-start | bytes 1474564
  160.9 63.8 %copy-start.61 = (f32[512]{0:T(512)S(1)}, f32[512]{0:T(512)}, u32[]{:S(2)}) copy-start(f32[512]{0:T(512)} %param.39) | copy-start | bytes 6148
  222.9 3.0 copy-start.11
  223.6 2.1 copy-start.64
  223.6 2.3 copy-start.24
  224.7 108.4 %all-gather.5.cloned.1.call-start = ((), (), s32[]{:S(2)}) async-start(), calls=%async_computation.2 | async-start | bytes 8110080 | tf_op jit(solution)/shard_map/all_gather | solution.py:219
  225.6 369.1 %reduce-scatter.2.cloned.1.call-start = ((), (), s32[]{:S(2)}) async-start(), calls=%async_computation.3 | async-start | bytes 16220160 | tf_op jit(solution)/shard_map/reduce_scatter | solution.py:269
  484.4 488.8 %all-reduce.14.cloned.1.call-start = ((), (), s32[]{:S(2)}) async-start(), calls=%async_computation.4 | async-start | bytes 13631488 | tf_op jit(solution)/shard_map/psum | solution.py:346
  497.4 19.0 %copy-start.12 = (bf16[2,6,40,256]{3,2,1,0:T(8,128)(2,1)S(1)}, bf16[2,6,40,256]{3,2,1,0:T(8,128)(2,1)}, u32[]{:S(2)}) copy-start(bf16[2,6,40,256]{3,2,1,0:T(8,128)(2,1)} %copy-done.11) | copy-start | bytes 737284
  497.4 97.3 %copy-start.27 = (bf16[256,768]{1,0:T(8,128)(2,1)S(1)}, bf16[256,768]{1,0:T(8,128)(2,1)}, u32[]{:S(2)}) copy-start(bf16[256,768]{1,0:T(8,128)(2,1)} %param.38) | copy-start | bytes 1179652
  497.4 97.3 %copy-start.51 = (f32[256]{0:T(256)S(1)}, f32[256]{0:T(256)}, u32[]{:S(2)}) copy-start(f32[256]{0:T(256)} %param.36) | copy-start | bytes 3076
  516.2 80.0 %copy-start.2 = (f32[2,6,40,256]{3,2,1,0:T(8,128)S(1)}, f32[2,6,40,256]{3,2,1,0:T(8,128)}, u32[]{:S(2)}) copy-start(f32[2,6,40,256]{3,2,1,0:T(8,128)} %copy-done.1) | copy-start | bytes 1474564
  516.3 80.0 %copy-start.31 = (f32[2,256]{1,0:T(2,128)S(1)}, f32[2,256]{1,0:T(2,128)}, u32[]{:S(2)}) copy-start(f32[2,256]{1,0:T(2,128)} %copy-done.30) | copy-start | bytes 6148
  516.3 80.0 %copy-start.33 = (f32[2,256]{1,0:T(2,128)S(1)}, f32[2,256]{1,0:T(2,128)}, u32[]{:S(2)}) copy-start(f32[2,256]{1,0:T(2,128)} %copy-done.32) | copy-start | bytes 6148
  516.4 144.6 %copy-start.49 = (f32[2]{0:T(128)S(1)}, f32[2]{0:T(128)}, u32[]{:S(2)}) copy-start(f32[2]{0:T(128)} %copy-done.48) | copy-start | bytes 28
  516.4 145.0 %copy-start.10 = (bf16[2,6,40,256]{3,2,1,0:T(8,128)(2,1)S(1)}, bf16[2,6,40,256]{3,2,1,0:T(8,128)(2,1)}, u32[]{:S(2)}) copy-start(bf16[2,6,40,256]{3,2,1,0:T(8,128)(2,1)} %param.23) | copy-start | bytes 737284
  661.8 8.6 copy-start.22
  661.8 8.6 copy-start.29
  665.8 5.9 collective-permute-start.4
  667.7 5.3 collective-permute-start.5
  673.2 1.4 copy-start.19
  673.2 1.4 copy-start.39
  673.2 1.4 copy-start.41
  673.2 1.4 copy-start.43
  673.2 1.4 copy-start.47
  673.2 1.4 copy-start.55
  673.2 1.4 copy-start.57
  737.4 9.9 %collective-permute-start.6 = (bf16[2,1,40,256]{3,2,1,0:T(8,128)(2,1)S(1)}, bf16[2,1,40,256]{3,2,1,0:T(8,128)(2,1)S(1)}, u32[]{:S(2)}, u32[]{:S(2)}) collective-permute-start(bf16[2,1,40,256]{3,2,1,0:T(8,128)(2,1)S(1)} %get-tuple-element.87), channel_id=1, source_target_pairs={{0,1},{1,2},{2,3},{3,4},{4,5},{5,6},{6,7},{7,8},{8,9},{9,10},{10,1... | collective-permute-start | bytes 122888 | tf_op jit(solution)/shard_map/ppermute | solution.py:19
  739.3 8.0 collective-permute-start.7
  747.5 1.4 copy-start.18
  747.5 1.4 copy-start.35
  747.5 1.4 copy-start.37
  747.5 1.4 copy-start.53
  748.9 64.5 %copy-start.45 = (bf16[2,512]{1,0:T(2,128)(2,1)S(1)}, bf16[2,512]{1,0:T(2,128)(2,1)}, u32[]{:S(2)}) copy-start(bf16[2,512]{1,0:T(2,128)(2,1)} %param.22) | copy-start | bytes 6148
  814.8 2.7 copy-start.60
  973.2 3.4 copy-start.20
  973.2 4.4 copy-start.8
  977.6 1.7 copy-start.23
  977.6 2.6 copy-start.28
  (15 other events, 16.1 us)
Sparse Core Ops, SparseCore 0:
  224.8 51.5 all-gather.2
  279.3 51.1 all-gather.4
  484.5 110.1 reduce-scatter.1
  814.9 158.2 all-reduce.13
where the time goes:
time: 995 us; the launch traced here: 988 us
  blocking collectives  439 us (44%)
  waiting for transfers between devices  219 us (22%)
  matrix products  171 us (17%)
  local copies, waits for them, and re-layouts  72.8 us (7%)
  other arithmetic  47.9 us (5%)
  starting transfers between devices  23.1 us (2%)
  between operations  15.5 us (2%)
    psum x5, blocking collectives, group_totals(): return lax.psum((first_part, second_part), 'seq')  313 us
    psum x1, waiting for transfers between devices, per_device(): lax.psum((gn1_gain_grad, gn1_bias_grad, conv1_weight_grad, conv1_bias_gra...  87.4 us
    reduce_scatter x1, waiting for transfers between devices, per_device(): lax.psum_scatter(jnp.concatenate([key_term, value_term], axis=2).reshape(...  77.3 us
    psum x1, blocking collectives, per_device(): lax.psum((gn1_gain_grad, gn1_bias_grad, conv1_weight_grad, conv1_bias_gra...  65.2 us
    psum x1, blocking collectives, per_device(): lax.psum((first_part, second_part, scale_part, offset_part), 'seq')  60.6 us
    all_gather x1, waiting for transfers between devices, per_device(): lax.all_gather(keys_low, 'seq', axis=1, tiled=True)  50.1 us
    dot_general x1, matrix products, full_grads(): jnp.einsum('iqhd,ikhd->ihqk', grad_heads, value_heads, preferred_element_...  39.7 us
    dot_general x1, matrix products, per_device(): jnp.einsum('ihqk,iqhd->kihd', weights_low, grad_heads, preferred_element_...  25.9 us
  transfers between devices with their start and end apart: 12, of which 5 were waited for; matrix products, arithmetic and copies ran while one was open for 10% of the time, Pallas kernels for 0%

commit v1 on v0

--- a/solution.py
+++ b/solution.py
@@ -33,8 +33,23 @@
     return values.reshape(values.shape[0], -1, GROUPS, values.shape[-1] // GROUPS)
 
 
+def seq_shift(value, dx, dy, dc):
+    pairs = []
+    for place in range(32):
+        x, y, c = place // 8, place // 2 % 4, place % 2
+        pairs.append((place, (x + dx) % 4 * 8 + (y + dy) % 4 * 2 + (c + dc) % 2))
+    return lax.ppermute(value, "seq", pairs)
+
+
+def seq_total(value):
+    value = value + seq_shift(value, 0, 0, 1)
+    value = (value + seq_shift(value, 0, 2, 0)) + (seq_shift(value, 0, 1, 0) + seq_shift(value, 0, 3, 0))
+    return (value + seq_shift(value, 2, 0, 0)) + (seq_shift(value, 1, 0, 0) + seq_shift(value, 3, 0, 0))
+
+
 def group_totals(first_part, second_part):
-    return lax.psum((first_part, second_part), "seq")
+    both = seq_total(jnp.concatenate([first_part, second_part], axis=-1))
+    return both[:, :GROUPS], both[:, GROUPS:]
 
 
 def group_parts(values, normed):
@@ -312,8 +327,9 @@
     gn2_bias_grad = jnp.sum(base_grad, axis=(0, 1, 2))
     second_dhat = base_grad * gn2_gain
     first_part, second_part = group_parts(second_dhat, second_hat)
-    first_sum, second_sum, scale_total, offset_total = lax.psum(
-        (first_part, second_part, scale_part, offset_part), "seq"
+    sums = seq_total(jnp.concatenate([first_part, second_part, scale_part, offset_part], axis=-1))
+    first_sum, second_sum, scale_total, offset_total = jnp.split(
+        sums, (GROUPS, 2 * GROUPS, 2 * GROUPS + channels), axis=-1
     )
     hidden_grad = norm_input_grad(
         second_dhat, second_hat, second_spread, valid_mask, counts, first_sum, second_sum

time: 995 us -> 728 us (0.73)
  blocking collectives: 439 us -> 65.6 us
  starting transfers between devices: 23.1 us -> 102 us
  waiting for transfers between devices: 219 us -> 242 us
    psum x6 -> x0, blocking collectives: 374 us -> none  [the longest x5 313 us: group_totals(): return lax.psum((first_part, second_part), 'seq')]
    ppermute x0 -> x42, starting transfers between devices: none -> 75.6 us  [seq_shift(): return lax.ppermute(value, 'seq', pairs)]
    reduce_scatter x1, waiting for transfers between devices: 77.3 us -> 92.8 us  [per_device(): lax.psum_scatter(jnp.concatenate([key_term, value_term], axis=2).reshape(...]
    psum x1, waiting for transfers between devices: 87.4 us -> 72.6 us  [per_device(): lax.psum((gn1_gain_grad, gn1_bias_grad, conv1_weight_grad, conv1_bias_gra...]
    ppermute x0 -> x42, waiting for transfers between devices: none -> 12.5 us  [seq_shift(): return lax.ppermute(value, 'seq', pairs)]
  transfers between devices with their start and end apart: 12 -> 54, of which waited for: 5 -> 24; matrix products, arithmetic and copies ran while one was open for 10% -> 14% of each run, Pallas kernels for 0% -> 0%
where the time goes in v1:
time: 728 us; the launch traced here: 718 us
  waiting for transfers between devices  242 us (33%)
  matrix products  170 us (23%)
  starting transfers between devices  102 us (14%)
  local copies, waits for them, and re-layouts  71.9 us (10%)
  blocking collectives  65.6 us (9%)
  other arithmetic  50 us (7%)
  between operations  15.7 us (2%)
    reduce_scatter x1, waiting for transfers between devices, per_device(): lax.psum_scatter(jnp.concatenate([key_term, value_term], axis=2).reshape(...  92.8 us
    ppermute x42, starting transfers between devices, seq_shift(): return lax.ppermute(value, 'seq', pairs)  75.6 us
    psum x1, waiting for transfers between devices, per_device(): lax.psum((gn1_gain_grad, gn1_bias_grad, conv1_weight_grad, conv1_bias_gra...  72.6 us
    psum x1, blocking collectives, per_device(): lax.psum((gn1_gain_grad, gn1_bias_grad, conv1_weight_grad, conv1_bias_gra...  65.6 us
    all_gather x1, waiting for transfers between devices, per_device(): lax.all_gather(keys_low, 'seq', axis=1, tiled=True)  54.1 us
    dot_general x1, matrix products, full_grads(): jnp.einsum('iqhd,ikhd->ihqk', grad_heads, value_heads, preferred_element_...  39.5 us
    dot_general x1, matrix products, per_device(): jnp.einsum('ihqk,iqhd->kihd', weights_low, grad_heads, preferred_element_...  25.8 us
    dot_general x1, matrix products, attend_piece(): jnp.einsum('iqhd,ikhd->ihqk', query_heads, key_heads, preferred_element_t...  24.7 us
  transfers between devices with their start and end apart: 54, of which 24 were waited for; matrix products, arithmetic and copies ran while one was open for 14% of the time, Pallas kernels for 0%

profile of v1, /device:TPU:1, one launch (start us, length us, event | category | flops | bytes accessed | tf_op | source)
XLA Modules:
  0.0 717.6 jit_solution(8940196569159365104)
XLA Ops:
  10.5 1.4 collective-permute-start
  12.8 3.0 collective-permute-start.1
  16.2 2.3 collective-permute-start.3
  19.5 2.8 collective-permute-start.4
  22.6 2.4 collective-permute-start.6
  27.7 4.1 collective-permute-start.7
  31.9 2.2 collective-permute-start.8
  34.1 3.1 collective-permute-done.8
  41.1 4.9 collective-permute-start.10
  46.1 2.6 collective-permute-start.12
  49.6 3.9 collective-permute-start.13
  53.6 2.7 collective-permute-start.15
  58.0 4.9 collective-permute-start.16
  62.9 1.9 collective-permute-start.17
  64.9 3.4 collective-permute-done.17
  72.2 2.7 collective-permute-start.19
  76.0 1.6 collective-permute-start.21
  78.6 5.5 collective-permute-start.22
  84.1 3.0 collective-permute-start.24
  92.5 54.1 %all-gather.3.cloned.1.call-done = bf16[2,7680,256]{2,1,0:T(8,128)(2,1)} async-done(((bf16[2,240,256]{2,1,0:T(8,128)(2,1)}), bf16[2,7680,256]{2,1,0:T(8,128)(2,1)}) %all-gather.3.cloned.1.call-update) | async-done | bytes 7864336 | tf_op jit(solution)/shard_map/all_gather | solution.py:233
  146.6 10.7 %copy.53 = bf16[2,7680,256]{1,2,0:T(8,128)(2,1)} copy(bf16[2,7680,256]{2,1,0:T(8,128)(2,1)} %all-gather.3.cloned.1.call-done) | data formatting | bytes 15728640 | tf_op jit(solution)/shard_map/all_gather | solution.py:233
  157.3 24.7 %fusion.3 = (f32[2,4,240]{2,1,0:T(4,128)S(1)}, f32[2,4,240,7680]{3,2,1,0:T(8,128)}) fusion(pred[2,7680]{1,0:T(4,128)(4,1)S(1)} %compare_and_fusion, bf16[2,240,4,64]{1,3,2,0:T(8,128)(2,1)S(1)} %bitcast.122, bf16[2,7680,4,64]{1,3,2,0:T(8,128)(2,1)} %bitcast.113), kind=kOutput, calls=%fused_computation.7 | convolution fusion | flops 1931671680 | bytes 67115520 | tf_op jit(solution)/shard_map/iqhd,ikhd->ihqk/dot_general | solution.py:133
  182.0 21.0 %fusion = f32[2,4,240]{2,1,0:T(4,128)S(1)} fusion(f32[2,4,240,7680]{3,2,1,0:T(8,128)} %get-tuple-element.95, f32[2,4,240]{2,1,0:T(4,128)S(1)} %broadcast_maximum_fusion, pred[2,7680]{1,0:T(4,128)(4,1)S(1)} %compare_and_fusion), kind=kLoop, calls=%fused_computation.4 | loop fusion | flops 73726080 | bytes 59013120 | tf_op jit(solution)/shard_map/reduce_sum | solution.py:139
  203.1 10.3 %copy.54 = bf16[2,7680,256]{1,2,0:T(8,128)(2,1)} copy(bf16[2,7680,256]{2,1,0:T(8,128)(2,1)} %all-gather.5.cloned.1.call-done) | data formatting | bytes 15728640 | tf_op jit(solution)/shard_map/all_gather | solution.py:234
  213.3 24.3 %multiply_reduce_fusion = (f32[2,240,4]{1,2,0:T(4,128)S(1)}, bf16[2,240,4,64]{1,3,2,0:T(8,128)(2,1)}) fusion(bf16[2,240,256]{1,2,0:T(8,128)(2,1)S(1)} %copy.56, f32[2,240,4]{1,2,0:T(4,128)S(1)} %bitcast.142, bf16[2,7680,4,64]{1,3,2,0:T(8,128)(2,1)} %bitcast.116, f32[2,4,240,7680]{3,2,1,0:T(8,128)} %get-tuple-element.95, ...), kind=kOutput, calls=%fused_computation.46 | convolution fusion | flops 1961777280 | bytes 67376640 | tf_op jit(solution)/shard_map/ihqk,ikhd->ihqd/dot_general | solution.py:140
  237.6 25.8 %fusion.14 = bf16[7680,2,4,64]{0,3,2,1:T(8,128)(2,1)} fusion(bf16[2,240,4,64]{1,3,2,0:T(8,128)(2,1)S(1)} %bitcast.137, f32[2,4,240,7680]{3,2,1,0:T(8,128)} %get-tuple-element.95, f32[2,4,240]{2,1,0:T(4,128)S(1)} %log_add_fusion, pred[2,7680]{1,0:T(4,128)(4,1)S(1)} %compare_and_fusion), kind=kOutput, calls=%fused_computation.16 | convolution fusion | flops 1965096960 | bytes 67115520 | tf_op jit(solution)/shard_map/ihqk,iqhd->kihd/dot_general | solution.py:280
  263.4 39.5 %multiply_convert_fusion = bf16[2,4,240,7680]{3,2,1,0:T(8,128)(2,1)} fusion(f32[2,4,240,7680]{3,2,1,0:T(8,128)} %get-tuple-element.95, f32[2,4,240]{2,1,0:T(4,128)S(1)} %bitcast.143, f32[2,4,240]{2,1,0:T(4,128)S(1)} %log_add_fusion, pred[2,7680]{1,0:T(4,128)(4,1)S(1)} %compare_and_fusion, bf16[2,240,4,64]{1,3,2,0:T(8,128)(2,1)S(1)} %bitcast.138, ...), kind=kOutput, calls=%fused_computation | convolution fusion | flops 2005401600 | bytes 96614400 | tf_op jit(solution)/shard_map/iqhd,ikhd->ihqk/dot_general | solution.py:157
  302.9 17.8 %fusion.13 = bf16[7680,2,4,64]{0,3,2,1:T(8,128)(2,1)} fusion(bf16[2,240,4,64]{1,3,2,0:T(8,128)(2,1)S(1)} %bitcast.123, bf16[2,4,240,7680]{3,2,1,0:T(8,128)(2,1)} %multiply_convert_fusion), kind=kOutput, calls=%fused_computation.15 | convolution fusion | flops 1891368960 | bytes 37601280 | tf_op jit(solution)/shard_map/ihqk,iqhd->kihd/dot_general | solution.py:277
  320.7 13.3 %pad_maximum_fusion = bf16[7680,2,8,64]{0,3,2,1:T(8,128)(2,1)} fusion(bf16[7680,2,4,64]{0,3,2,1:T(8,128)(2,1)} %fusion.14, bf16[7680,2,4,64]{0,3,2,1:T(8,128)(2,1)} %fusion.13), kind=kLoop, calls=%fused_computation.12 | loop fusion | flops 7864320 | bytes 31457280 | tf_op jit(solution)/shard_map/concatenate | solution.py:285
  334.0 20.7 %copy.57 = bf16[7680,2,512]{2,0,1:T(8,128)(2,1)} copy(bf16[7680,2,512]{0,2,1:T(8,128)(2,1)} %bitcast.115) | data formatting | bytes 31457280 | tf_op jit(solution)/shard_map/convert_element_type | solution.py:287
  355.5 16.8 %convert_reduce_fusion = (f32[4,64]{1,0:T(4,128)S(1)}, bf16[2,4,64,240]{3,2,1,0:T(8,128)(2,1)S(1)}) fusion(bf16[2,7680,4,64]{1,3,2,0:T(8,128)(2,1)} %bitcast.114, bf16[2,4,240,7680]{3,2,1,0:T(8,128)(2,1)} %multiply_convert_fusion), kind=kOutput, calls=%fused_computation.45 | convolution fusion | flops 1887805184 | bytes 37602304 | tf_op jit(solution)/shard_map/ihqk,ikhd->iqhd/dot_general | solution.py:271
  372.5 92.8 %reduce-scatter.2.cloned.1.call-done = bf16[240,2,512]{2,0,1:T(8,128)(2,1)} async-done(((bf16[7680,2,512]{2,0,1:T(8,128)(2,1)}), bf16[240,2,512]{2,0,1:T(8,128)(2,1)}) %reduce-scatter.2.cloned.1.call-update) | async-done | bytes 491536 | tf_op jit(solution)/shard_map/reduce_scatter | solution.py:284
  465.3 1.5 multiply_reduce_fusion.12
  468.3 2.0 collective-permute-start.25
  471.2 1.6 copy.60
  475.0 7.0 dot_general.88
  482.1 2.4 collective-permute-start.26
  485.1 2.1 collective-permute-start.28
  489.9 2.1 collective-permute-start.31
  493.9 5.0 collective-permute-start.32
  499.0 1.9 collective-permute-start.33
  500.9 2.3 convolution_bitcast_fusion
  505.9 1.9 multiply_reduce_fusion.2
  509.5 3.6 collective-permute-start.35
  513.1 1.5 collective-permute-start.36
  517.1 3.7 collective-permute-start.38
  520.8 2.7 collective-permute-start.40
  523.5 3.9 fusion.91
  529.1 4.1 fusion.19
  533.3 1.3 convolution_select_fusion
  534.6 4.4 collective-permute-start.41
  539.0 2.2 collective-permute-start.42
  542.1 2.3 collective-permute-done.42
  545.9 1.8 multiply_reduce_fusion.3
  549.4 2.4 collective-permute-start.44
  551.8 1.5 collective-permute-start.45
  554.5 1.3 collective-permute-done.45
  556.1 3.3 collective-permute-start.47
  559.4 2.7 collective-permute-start.49
  562.1 65.6 %all-reduce.4 = (f32[256]{0:T(256)}, f32[256]{0:T(256)}, f32[256]{0:T(256)}, f32[512]{0:T(512)}, f32[256]{0:T(256)}, /*index=5*/f32[256]{0:T(256)}, f32[256]{0:T...) all-reduce(f32[256]{0:T(256)S(1)} %get-tuple-element.24, ...), channel_id=1, replica_groups=mesh['dp'=4,'seq'=32] {'dp','seq'}, use_global_device_ids=true, to_apply=%region_31.32 | all-reduce | flops 3328 | bytes 26624 | tf_op jit(solution)/shard_map/psum | solution.py:362
  628.1 2.3 multiply_convert_fusion.1
  630.4 72.6 %all-reduce.8.cloned.1.call-done = (f32[3,3,256,256]{3,2,1,0:T(8,128)}, f32[512,512]{1,0:T(8,128)}, f32[3,3,256,256]{3,2,1,0:T(8,128)}, f32[256,768]{1,0:T(8,128)}, f32[256,256]{1,0:T(8,128)}) async-done(((f32[3,3,256,256]{3,2,1,0:T(8,128)}, f32[512,512]{1,0:T(8,128)}, f32[3,3,256,256]{3,2,1,0:T(8,128)}, f32[256,768]{1,0:T(8,128)}, f32[256,256]{1,0:T(8,128)}), (f32[3,3,256,256]{3,2,1,0:T(8,128)}, ...) | async-done | bytes 6815760 | tf_op jit(solution)/shard_map/psum | solution.py:362
  703.0 3.4 copy.113
  707.4 1.4 copy.115
  (384 shorter events, 54.1 us)
Async XLA Ops:
  7.2 41.5 %copy-start = (bf16[512,512]{1,0:T(8,128)(2,1)S(1)}, bf16[512,512]{1,0:T(8,128)(2,1)}, u32[]{:S(2)}) copy-start(bf16[512,512]{1,0:T(8,128)(2,1)} %param.30) | copy-start | bytes 1572868
  7.2 139.3 %all-gather.3.cloned.1.call-start = ((), (), s32[]{:S(2)}) async-start(), calls=%async_computation.1 | async-start | bytes 8110080 | tf_op jit(solution)/shard_map/all_gather | solution.py:233
  9.0 79.3 %copy-start.15 = (f32[2,6,40]{2,1,0:T(8,128)}, f32[2,6,40]{2,1,0:T(8,128)S(1)}, u32[]{:S(2)}) copy-start(f32[2,6,40]{2,1,0:T(8,128)S(1)} %and_convert_fusion) | copy-start | bytes 5764
  10.5 2.3 collective-permute-start
  12.8 5.7 collective-permute-start.1
  15.8 3.6 collective-permute-start.2
  16.2 3.2 collective-permute-start.3
  19.5 6.2 collective-permute-start.4
  22.3 3.7 collective-permute-start.5
  22.6 3.4 collective-permute-start.6
  25.7 62.1 %copy-start.53 = (f32[2]{0:T(128)}, f32[2]{0:T(128)S(1)}, u32[]{:S(2)}) copy-start(f32[2]{0:T(128)S(1)} %convert_multiply_fusion.4) | copy-start | bytes 28
  27.7 6.3 collective-permute-start.7
  31.9 5.3 collective-permute-start.8
  39.9 1.2 collective-permute-start.9
  41.1 7.7 %collective-permute-start.10 = (f32[2,64]{1,0:T(2,128)S(1)}, f32[2,64]{1,0:T(2,128)S(1)}, u32[]{:S(2)}, u32[]{:S(2)}) collective-permute-start(f32[2,64]{1,0:T(2,128)S(1)} %fusion.124), channel_id=1, source_target_pairs={{0,4},{1,5},{2,6},{3,7},{4,0},{5,1},{6,2},{7,3},{8,12},{9,13},{10,... | collective-permute-start | bytes 1544 | tf_op jit(solution)/shard_map/ppermute | solution.py:41
  46.0 3.6 collective-permute-start.11
  46.1 3.5 collective-permute-start.12
  49.6 6.6 collective-permute-start.13
  53.6 3.6 collective-permute-start.14
  53.6 3.6 collective-permute-start.15
  58.0 6.9 collective-permute-start.16
  62.9 5.3 collective-permute-start.17
  71.0 1.2 collective-permute-start.18
  72.2 5.4 collective-permute-start.19
  74.9 3.6 collective-permute-start.20
  76.0 2.5 collective-permute-start.21
  78.6 8.5 %collective-permute-start.22 = (f32[2,64]{1,0:T(2,128)S(1)}, f32[2,64]{1,0:T(2,128)S(1)}, u32[]{:S(2)}, u32[]{:S(2)}) collective-permute-start(f32[2,64]{1,0:T(2,128)S(1)} %add_add_fusion.7), channel_id=1, source_target_pairs={{0,16},{1,17},{2,18},{3,19},{4,20},{5,21},{6,22},{7,23},{8,24},{9,... | collective-permute-start | bytes 1544 | tf_op jit(solution)/shard_map/ppermute | solution.py:41
  84.1 3.6 collective-permute-start.23
  84.1 3.7 collective-permute-start.24
  90.9 112.2 %all-gather.5.cloned.1.call-start = ((), (), s32[]{:S(2)}) async-start(), calls=%async_computation.2 | async-start | bytes 8110080 | tf_op jit(solution)/shard_map/all_gather | solution.py:234
  91.7 373.6 %reduce-scatter.2.cloned.1.call-start = ((), (), s32[]{:S(2)}) async-start(), calls=%async_computation.3 | async-start | bytes 16220160 | tf_op jit(solution)/shard_map/reduce_scatter | solution.py:284
  354.7 348.3 %all-reduce.8.cloned.1.call-start = ((), (), s32[]{:S(2)}) async-start(), calls=%async_computation.4 | async-start | bytes 13631488 | tf_op jit(solution)/shard_map/psum | solution.py:362
  355.5 109.9 %copy-start.30 = (bf16[256,768]{1,0:T(8,128)(2,1)S(1)}, bf16[256,768]{1,0:T(8,128)(2,1)}, u32[]{:S(2)}) copy-start(bf16[256,768]{1,0:T(8,128)(2,1)} %param.38) | copy-start | bytes 1179652
  355.5 109.9 %copy-start.56 = (f32[256]{0:T(256)S(1)}, f32[256]{0:T(256)}, u32[]{:S(2)}) copy-start(f32[256]{0:T(256)} %param.36) | copy-start | bytes 3076
  372.3 95.3 %copy-start.2 = (f32[2,6,40,256]{3,2,1,0:T(8,128)S(1)}, f32[2,6,40,256]{3,2,1,0:T(8,128)}, u32[]{:S(2)}) copy-start(f32[2,6,40,256]{3,2,1,0:T(8,128)} %copy-done.1) | copy-start | bytes 1474564
  372.3 95.3 %copy-start.35 = (f32[2,256]{1,0:T(2,128)S(1)}, f32[2,256]{1,0:T(2,128)}, u32[]{:S(2)}) copy-start(f32[2,256]{1,0:T(2,128)} %copy-done.34) | copy-start | bytes 6148
  372.3 95.3 %copy-start.37 = (f32[2,256]{1,0:T(2,128)S(1)}, f32[2,256]{1,0:T(2,128)}, u32[]{:S(2)}) copy-start(f32[2,256]{1,0:T(2,128)} %copy-done.36) | copy-start | bytes 6148
  372.3 97.9 %copy-start.18 = (bf16[3,3,256,256]{3,2,1,0:T(8,128)(2,1)S(1)}, bf16[3,3,256,256]{3,2,1,0:T(8,128)(2,1)}, u32[]{:S(2)}) copy-start(bf16[3,3,256,256]{3,2,1,0:T(8,128)(2,1)} %param.34) | copy-start | bytes 3538948
  372.5 95.8 %copy-start.32 = (bf16[2,240,256]{2,1,0:T(8,128)(2,1)}, bf16[2,240,256]{2,1,0:T(8,128)(2,1)S(1)}, u32[]{:S(2)}) copy-start(bf16[2,240,256]{2,1,0:T(8,128)(2,1)S(1)} %copy.58) | copy-start | bytes 737284
  468.3 13.8 %collective-permute-start.25 = (f32[2,64]{1,0:T(2,128)S(1)}, f32[2,64]{1,0:T(2,128)S(1)}, u32[]{:S(2)}, u32[]{:S(2)}) collective-permute-start(f32[2,64]{1,0:T(2,128)S(1)} %pad_maximum_fusion.17), channel_id=1, source_target_pairs={{0,1},{1,0},{2,3},{3,2},{4,5},{5,4},{6,7},{7,6},{8,9},{9,8},{10,11... | collective-permute-start | bytes 1544 | tf_op jit(solution)/shard_map/ppermute | solution.py:41
  482.1 5.3 collective-permute-start.26
  484.5 3.6 collective-permute-start.27
  485.1 3.1 collective-permute-start.28
  488.1 5.0 collective-permute-start.29
  489.4 3.7 collective-permute-start.30
  489.9 3.2 collective-permute-start.31
  493.9 9.3 %collective-permute-start.32 = (bf16[2,1,40,256]{3,2,1,0:T(8,128)(2,1)S(1)}, bf16[2,1,40,256]{3,2,1,0:T(8,128)(2,1)S(1)}, u32[]{:S(2)}, u32[]{:S(2)}) collective-permute-start(bf16[2,1,40,256]{3,2,1,0:T(8,128)(2,1)S(1)} %get-tuple-element.75), channel_id=1, source_target_pairs={{0,1},{1,2},{2,3},{3,4},{4,5},{5,6},{6,7},{7,8},{8,9},{9,10},{10,1... | collective-permute-start | bytes 122888 | tf_op jit(solution)/shard_map/ppermute | solution.py:19
  499.0 5.3 collective-permute-start.33
  508.2 1.2 collective-permute-start.34
  509.5 6.3 collective-permute-start.35
  513.1 3.7 collective-permute-start.36
  514.6 2.5 collective-permute-start.37
  517.1 10.3 %collective-permute-start.38 = (f32[2,576]{1,0:T(2,128)S(1)}, f32[2,576]{1,0:T(2,128)S(1)}, u32[]{:S(2)}, u32[]{:S(2)}) collective-permute-start(f32[2,576]{1,0:T(2,128)S(1)} %add_add_fusion.1), channel_id=1, source_target_pairs={{0,16},{1,17},{2,18},{3,19},{4,20},{5,21},{6,22},{7,23},{8,24},{9,... | collective-permute-start | bytes 13832 | tf_op jit(solution)/shard_map/ppermute | solution.py:41
  520.8 6.6 collective-permute-start.39
  520.8 6.6 collective-permute-start.40
  534.6 7.5 %collective-permute-start.41 = (bf16[2,1,40,256]{3,2,1,0:T(8,128)(2,1)S(1)}, bf16[2,1,40,256]{3,2,1,0:T(8,128)(2,1)S(1)}, u32[]{:S(2)}, u32[]{:S(2)}) collective-permute-start(bf16[2,1,40,256]{3,2,1,0:T(8,128)(2,1)S(1)} %get-tuple-element.73), channel_id=1, source_target_pairs={{0,1},{1,2},{2,3},{3,4},{4,5},{5,6},{6,7},{7,8},{8,9},{9,10},{10,1... | collective-permute-start | bytes 122888 | tf_op jit(solution)/shard_map/ppermute | solution.py:19
  539.0 5.3 collective-permute-start.42
  548.2 1.2 collective-permute-start.43
  549.4 5.1 collective-permute-start.44
  551.8 4.0 collective-permute-start.45
  553.3 2.8 collective-permute-start.46
  556.1 71.6 %collective-permute-start.47 = (f32[2,64]{1,0:T(2,128)S(1)}, f32[2,64]{1,0:T(2,128)S(1)}, u32[]{:S(2)}, u32[]{:S(2)}) collective-permute-start(f32[2,64]{1,0:T(2,128)S(1)} %add_add_fusion.3), channel_id=1, source_target_pairs={{0,16},{1,17},{2,18},{3,19},{4,20},{5,21},{6,22},{7,23},{8,24},{9,... | collective-permute-start | bytes 1544 | tf_op jit(solution)/shard_map/ppermute | solution.py:41
  559.4 68.2 %collective-permute-start.48 = (f32[2,64]{1,0:T(2,128)S(1)}, f32[2,64]{1,0:T(2,128)S(1)}, u32[]{:S(2)}, u32[]{:S(2)}) collective-permute-start(f32[2,64]{1,0:T(2,128)S(1)} %add_add_fusion.3), channel_id=1, source_target_pairs={{0,8},{1,9},{2,10},{3,11},{4,12},{5,13},{6,14},{7,15},{8,16},{9,17... | collective-permute-start | bytes 1544 | tf_op jit(solution)/shard_map/ppermute | solution.py:41
  559.4 68.2 %collective-permute-start.49 = (f32[2,64]{1,0:T(2,128)S(1)}, f32[2,64]{1,0:T(2,128)S(1)}, u32[]{:S(2)}, u32[]{:S(2)}) collective-permute-start(f32[2,64]{1,0:T(2,128)S(1)} %add_add_fusion.3), channel_id=1, source_target_pairs={{0,24},{1,25},{2,26},{3,27},{4,28},{5,29},{6,30},{7,31},{8,0},{9,1... | collective-permute-start | bytes 1544 | tf_op jit(solution)/shard_map/ppermute | solution.py:41
  (63 other events, 583.7 us)
Sparse Core Ops, SparseCore 0:
  91.0 55.5 all-gather.2
  149.4 51.1 all-gather.4
  354.8 110.4 reduce-scatter.1
  542.2 160.7 all-reduce.7
